TPU v7x, 32 devices: a whole 2x2x4 slice. The times are simulated.
32 devices in a mesh: depth: 4 (over x, core), row: 4 (over z), col: 2 (over y).
Axes of the slice: x: 2, y: 2, z: 4, core: 2. Of those that a mesh axis runs over, the one named last changes fastest.
Arguments:
- density: float32 [4096, 4096], P('row', ('depth', 'col')), as said below
- pattern: int32 [64, 64], replicated, may hold values from 0 to 1, as said below
- filters: int32 [4, 64, 64], replicated, may hold values from 0 to 1, as said below
Outputs:
- purified: float32 [4096, 4096], P('row', ('depth', 'col'))
Inputs may be any that keep to these rules, and one draw needn't show every extreme that they name: density is symmetric. `pattern`: symmetric 0/1 block table with every diagonal block set. `filters`: each table is a symmetric 0/1 block table with every diagonal block set.
All inputs are finite; a program needn't handle non-finite values.
Results may differ from a plain program's by a relative error of at most 0.007.
Values may be sent and summed in bfloat16 or wider, within the bound.
A program may use at most 64 MiB of HBM per device.

v0:
```python
import jax
import jax.numpy as jnp
from jax import lax
from jax.sharding import PartitionSpec as P

BLK = 64
PURIFY = 2


def spread(value, axis, root):
    mine = lax.axis_index(axis) == root
    return lax.psum(jnp.where(mine, value, jnp.zeros_like(value)), axis)


def on_device(density, pattern, filters):
    rows_wide, seg_width = density.shape
    n_depth = lax.axis_size("depth")
    n_col = lax.axis_size("col")
    layer_index = lax.axis_index("depth")
    row_index = lax.axis_index("row")
    col_index = lax.axis_index("col")
    row_blocks = rows_wide // BLK
    seg_blocks = seg_width // BLK

    def full_mask(keep_table):
        row_strip = lax.dynamic_slice_in_dim(keep_table, row_index * row_blocks, row_blocks, 0)
        groups = row_strip.reshape(row_blocks, n_depth, n_col, seg_blocks)
        picked = lax.dynamic_slice_in_dim(groups, col_index, 1, 2)
        return picked.reshape(row_blocks, n_depth * seg_blocks).astype(jnp.float32)

    def own_mask(keep_table):
        return lax.dynamic_slice_in_dim(
            full_mask(keep_table), layer_index * seg_blocks, seg_blocks, 1
        )

    def apply_mask(values, keep_mask):
        row_count, col_count = keep_mask.shape
        shaped = values.reshape(row_count, BLK, col_count, BLK) * keep_mask[:, None, :, None]
        return shaped.reshape(values.shape)

    def multiply(left_tile, right_side):
        return jnp.dot(
            lax.all_gather(left_tile, "col", axis=1, tiled=True),
            right_side,
            preferred_element_type=jnp.float32,
        )

    def share_layers(partial_sum):
        return lax.psum_scatter(partial_sum, "depth", scatter_dimension=1, tiled=True)

    start_matrix = apply_mask(density, own_mask(pattern))
    current = start_matrix
    for round_index in range(PURIFY):
        operand = current.astype(jnp.bfloat16)
        right_side = spread(
            lax.all_gather(operand, "depth", axis=1, tiled=True), "row", layer_index
        )
        square = apply_mask(
            share_layers(multiply(operand, right_side)), own_mask(filters[2 * round_index])
        )
        cubic = apply_mask(
            share_layers(multiply(square.astype(jnp.bfloat16), right_side)),
            own_mask(filters[2 * round_index + 1]),
        )
        current = 3.0 * square - 2.0 * cubic
    return current


def solution(mesh):
    return jax.shard_map(
        on_device,
        mesh=mesh,
        in_specs=(P("row", ("depth", "col")), P(), P()),
        out_specs=P("row", ("depth", "col")),
        check_vma=False,
    )
```

profile of v0, /device:TPU:0, one launch (start us, length us, event | category | flops | bytes accessed | tf_op | source)
XLA Modules:
  0.0 889.9 jit_solution(13428316623293829066)
XLA Ops:
  7.5 2.3 mul.83
  9.8 3.4 mul.84
  13.2 2.9 multiply_convert_fusion
  16.9 36.5 %all-gather.9.cloned.1.call-done = bf16[1024,2048]{1,0:T(8,128)(2,1)} async-done(((bf16[1024,512]{1,0:T(8,128)(2,1)}), bf16[1024,2048]{1,0:T(8,128)(2,1)}) %all-gather.9.cloned.1.call-update) | async-done | bytes 4194320 | tf_op jit(solution)/shard_map/all_gather | solution.py:56
  53.5 4.5 broadcast_select_fusion.1
  58.0 30.2 %all-gather.7.cloned.1.call-done = bf16[1024,1024]{1,0:T(8,128)(2,1)} async-done(((bf16[1024,512]{1,0:T(8,128)(2,1)}), bf16[1024,1024]{1,0:T(8,128)(2,1)}) %all-gather.7.cloned.1.call-update) | async-done | bytes 2097168 | tf_op jit(solution)/shard_map/all_gather | solution.py:43
  88.2 157.4 %all-reduce.3.cloned.1.call-done = bf16[1024,2048]{1,0:T(8,128)(2,1)} async-done(((bf16[1024,2048]{1,0:T(8,128)(2,1)}), bf16[1024,2048]{1,0:T(8,128)(2,1)}) %all-reduce.3.cloned.1.call-update) | async-done | bytes 4194320 | tf_op jit(solution)/shard_map/psum | solution.py:12
  245.5 10.6 %fusion.1 = f32[1024,2048]{1,0:T(8,128)} fusion(bf16[1024,1024]{1,0:T(8,128)(2,1)} %all-gather.7.cloned.1.call-done, bf16[1024,2048]{1,0:T(8,128)(2,1)} %all-reduce.3.cloned.1.call-done), kind=kOutput, calls=%fused_computation.23 | convolution fusion | flops 4294967296 | bytes 14680064 | tf_op jit(solution)/shard_map/dot_general | solution.py:42
  257.2 2.3 mul.86
  259.5 3.8 mul.87
  263.3 63.7 %reduce-scatter.5.cloned.1.call-done = f32[1024,512]{1,0:T(8,128)} async-done(((f32[1024,2048]{1,0:T(8,128)}), f32[1024,512]{1,0:T(8,128)}) %reduce-scatter.5.cloned.1.call-update) | async-done | bytes 2097168 | tf_op jit(solution)/shard_map/reduce_scatter | solution.py:49
  327.0 2.9 multiply_convert_fusion.2
  330.0 33.2 %all-gather.11.cloned.1.call-done = bf16[1024,1024]{1,0:T(8,128)(2,1)} async-done(((bf16[1024,512]{1,0:T(8,128)(2,1)}), bf16[1024,1024]{1,0:T(8,128)(2,1)}) %all-gather.11.cloned.1.call-update) | async-done | bytes 2097168 | tf_op jit(solution)/shard_map/all_gather | solution.py:43
  363.2 10.6 %fusion.2 = f32[1024,2048]{1,0:T(8,128)} fusion(bf16[1024,1024]{1,0:T(8,128)(2,1)} %all-gather.11.cloned.1.call-done, bf16[1024,2048]{1,0:T(8,128)(2,1)} %all-reduce.3.cloned.1.call-done), kind=kOutput, calls=%fused_computation.24 | convolution fusion | flops 4294967296 | bytes 14680064 | tf_op jit(solution)/shard_map/dot_general | solution.py:42
  374.2 2.3 mul.90
  376.6 5.0 mul.91
  381.6 64.1 %reduce-scatter.7.cloned.1.call-done = f32[1024,512]{1,0:T(8,128)} async-done(((f32[1024,2048]{1,0:T(8,128)}), f32[1024,512]{1,0:T(8,128)}) %reduce-scatter.7.cloned.1.call-update) | async-done | bytes 2097168 | tf_op jit(solution)/shard_map/reduce_scatter | solution.py:49
  445.7 4.9 subtract_convert_fusion
  451.5 33.8 %all-gather.15.cloned.1.call-done = bf16[1024,2048]{1,0:T(8,128)(2,1)} async-done(((bf16[1024,512]{1,0:T(8,128)(2,1)}), bf16[1024,2048]{1,0:T(8,128)(2,1)}) %all-gather.15.cloned.1.call-update) | async-done | bytes 4194320 | tf_op jit(solution)/shard_map/all_gather | solution.py:56
  485.3 4.4 broadcast_select_fusion
  489.8 30.3 %all-gather.13.cloned.1.call-done = bf16[1024,1024]{1,0:T(8,128)(2,1)} async-done(((bf16[1024,512]{1,0:T(8,128)(2,1)}), bf16[1024,1024]{1,0:T(8,128)(2,1)}) %all-gather.13.cloned.1.call-update) | async-done | bytes 2097168 | tf_op jit(solution)/shard_map/all_gather | solution.py:43
  520.1 157.5 %all-reduce.5.cloned.1.call-done = bf16[1024,2048]{1,0:T(8,128)(2,1)} async-done(((bf16[1024,2048]{1,0:T(8,128)(2,1)}), bf16[1024,2048]{1,0:T(8,128)(2,1)}) %all-reduce.5.cloned.1.call-update) | async-done | bytes 4194320 | tf_op jit(solution)/shard_map/psum | solution.py:12
  677.6 10.6 %fusion.3 = f32[1024,2048]{1,0:T(8,128)} fusion(bf16[1024,1024]{1,0:T(8,128)(2,1)} %all-gather.13.cloned.1.call-done, bf16[1024,2048]{1,0:T(8,128)(2,1)} %all-reduce.5.cloned.1.call-done), kind=kOutput, calls=%fused_computation.25 | convolution fusion | flops 4294967296 | bytes 14680064 | tf_op jit(solution)/shard_map/dot_general | solution.py:42
  690.7 3.5 mul.95
  694.3 64.9 %reduce-scatter.9.cloned.1.call-done = f32[1024,512]{1,0:T(8,128)} async-done(((f32[1024,2048]{1,0:T(8,128)}), f32[1024,512]{1,0:T(8,128)}) %reduce-scatter.9.cloned.1.call-update) | async-done | bytes 2097168 | tf_op jit(solution)/shard_map/reduce_scatter | solution.py:49
  759.1 2.9 multiply_convert_fusion.1
  762.3 33.0 %all-gather.17.cloned.1.call-done = bf16[1024,1024]{1,0:T(8,128)(2,1)} async-done(((bf16[1024,512]{1,0:T(8,128)(2,1)}), bf16[1024,1024]{1,0:T(8,128)(2,1)}) %all-gather.17.cloned.1.call-update) | async-done | bytes 2097168 | tf_op jit(solution)/shard_map/all_gather | solution.py:43
  795.3 10.6 %fusion.4 = f32[1024,2048]{1,0:T(8,128)} fusion(bf16[1024,1024]{1,0:T(8,128)(2,1)} %all-gather.17.cloned.1.call-done, bf16[1024,2048]{1,0:T(8,128)(2,1)} %all-reduce.5.cloned.1.call-done), kind=kOutput, calls=%fused_computation.26 | convolution fusion | flops 4294967296 | bytes 14680064 | tf_op jit(solution)/shard_map/dot_general | solution.py:42
  806.1 2.3 mul.98
  808.4 5.0 mul.99
  813.4 64.4 %reduce-scatter.11.cloned.1.call-done = f32[1024,512]{1,0:T(8,128)} async-done(((f32[1024,2048]{1,0:T(8,128)}), f32[1024,512]{1,0:T(8,128)}) %reduce-scatter.11.cloned.1.call-update) | async-done | bytes 2097168 | tf_op jit(solution)/shard_map/reduce_scatter | solution.py:49
  877.8 5.2 multiply_subtract_fusion
  (55 shorter events, 7.2 us)
Async XLA Ops:
  6.5 0.8 copy-start
  6.5 46.9 %all-gather.9.cloned.1.call-start = ((), (), s32[]{:S(2)}) async-start(), calls=%async_computation.5 | async-start | bytes 5242880 | tf_op jit(solution)/shard_map/all_gather | solution.py:56
  16.1 72.0 %all-gather.7.cloned.1.call-start = ((), (), s32[]{:S(2)}) async-start(), calls=%async_computation.4 | async-start | bytes 3145728 | tf_op jit(solution)/shard_map/all_gather | solution.py:43
  16.9 228.7 %all-reduce.3.cloned.1.call-start = ((), (), s32[]{:S(2)}) async-start(), calls=%async_computation.6 | async-start | bytes 8388608 | tf_op jit(solution)/shard_map/psum | solution.py:12
  57.9 269.1 %reduce-scatter.5.cloned.1.call-start = ((), (), s32[]{:S(2)}) async-start(), calls=%async_computation.7 | async-start | bytes 10485760 | tf_op jit(solution)/shard_map/reduce_scatter | solution.py:49
  256.1 0.9 copy-start.2
  256.1 107.1 %all-gather.11.cloned.1.call-start = ((), (), s32[]{:S(2)}) async-start(), calls=%async_computation.8 | async-start | bytes 3145728 | tf_op jit(solution)/shard_map/all_gather | solution.py:43
  329.9 115.8 %reduce-scatter.7.cloned.1.call-start = ((), (), s32[]{:S(2)}) async-start(), calls=%async_computation.9 | async-start | bytes 10485760 | tf_op jit(solution)/shard_map/reduce_scatter | solution.py:49
  373.8 111.5 %all-gather.15.cloned.1.call-start = ((), (), s32[]{:S(2)}) async-start(), calls=%async_computation.11 | async-start | bytes 5242880 | tf_op jit(solution)/shard_map/all_gather | solution.py:56
  450.7 69.4 %all-gather.13.cloned.1.call-start = ((), (), s32[]{:S(2)}) async-start(), calls=%async_computation.10 | async-start | bytes 3145728 | tf_op jit(solution)/shard_map/all_gather | solution.py:43
  451.4 226.2 %all-reduce.5.cloned.1.call-start = ((), (), s32[]{:S(2)}) async-start(), calls=%async_computation.12 | async-start | bytes 8388608 | tf_op jit(solution)/shard_map/psum | solution.py:12
  489.8 269.4 %reduce-scatter.9.cloned.1.call-start = ((), (), s32[]{:S(2)}) async-start(), calls=%async_computation.13 | async-start | bytes 10485760 | tf_op jit(solution)/shard_map/reduce_scatter | solution.py:49
  688.2 107.1 %all-gather.17.cloned.1.call-start = ((), (), s32[]{:S(2)}) async-start(), calls=%async_computation.14 | async-start | bytes 3145728 | tf_op jit(solution)/shard_map/all_gather | solution.py:43
  762.1 115.8 %reduce-scatter.11.cloned.1.call-start = ((), (), s32[]{:S(2)}) async-start(), calls=%async_computation.15 | async-start | bytes 10485760 | tf_op jit(solution)/shard_map/reduce_scatter | solution.py:49
  877.8 5.2 copy-start.1
Sparse Core Ops, SparseCore 0:
  16.2 37.1 all-gather.8
  55.0 33.1 all-gather.6
  90.5 154.9 all-reduce.2
  256.3 70.7 reduce-scatter.4
  330.1 33.1 all-gather.10
  373.9 71.7 reduce-scatter.6
  450.8 34.4 all-gather.14
  486.9 33.1 all-gather.12
  522.6 154.9 all-reduce.4
  688.3 70.7 reduce-scatter.8
  762.2 33.1 all-gather.16
  806.1 71.7 reduce-scatter.10
where the time goes:
time: 891 us; the launch traced here: 890 us
  waiting for transfers between devices  771 us (87%)
  matrix products  42.3 us (5%)
  local copies, waits for them, and re-layouts  34.7 us (4%)
  other arithmetic  27.8 us (3%)
  between operations  13.7 us (2%)
    psum x2, waiting for transfers between devices, spread(): return lax.psum(jnp.where(mine, value, jnp.zeros_like(value)), axis)  315 us
    reduce_scatter x4, waiting for transfers between devices, share_layers(): lax.psum_scatter(partial_sum, 'depth', scatter_dimension=1, tiled=True)  257 us
    all_gather x4, waiting for transfers between devices, multiply(): lax.all_gather(left_tile, 'col', axis=1, tiled=True)  127 us
    all_gather x2, waiting for transfers between devices, on_device(): lax.all_gather(operand, 'depth', axis=1, tiled=True)  70.4 us
    dot_general x4, matrix products, multiply(): jnp.dot(lax.all_gather(left_tile, 'col', axis=1, tiled=True), right_side,...  42.3 us
    mul x10, local copies, waits for them, and re-layouts, apply_mask(): values.reshape(row_count, BLK, col_count, BLK) * keep_mask[:, None, :, None]  32.3 us
  transfers between devices with their start and end apart: 12, of which 12 were waited for; matrix products, arithmetic and copies ran while one was open for 4% of the time, Pallas kernels for 0%

commit v1 on v0

--- a/solution.py
+++ b/solution.py
@@ -7,9 +7,13 @@
 PURIFY = 2
 
 
+def rounds_launch(local, a_name):
+    return lax.all_gather(local, a_name).sum(axis=0)
+
+
 def spread(value, axis, root):
     mine = lax.axis_index(axis) == root
-    return lax.psum(jnp.where(mine, value, jnp.zeros_like(value)), axis)
+    return rounds_launch(jnp.where(mine, value, jnp.zeros_like(value)), axis)
 
 
 def on_device(density, pattern, filters):

time: 891 us -> 1160 us (1.30)
  waiting for transfers between devices: 771 us -> 1010 us
  other arithmetic: 27.8 us -> 52.6 us
    all_gather x0 -> x2, waiting for transfers between devices: none -> 572 us  [rounds_launch(): return lax.all_gather(local, a_name).sum(axis=0)]
    psum x2 -> x0, waiting for transfers between devices: 315 us -> none  [spread(): return lax.psum(jnp.where(mine, value, jnp.zeros_like(value)), axis)]
    reduce_sum x0 -> x2, other arithmetic: none -> 24.9 us  [rounds_launch(): return lax.all_gather(local, a_name).sum(axis=0)]
    all_gather x4, waiting for transfers between devices: 127 us -> 107 us  [multiply(): lax.all_gather(left_tile, 'col', axis=1, tiled=True)]
  transfers between devices with their start and end apart: 12 -> 12, of which waited for: 12 -> 12; matrix products, arithmetic and copies ran while one was open for 4% -> 5% of each run, Pallas kernels for 0% -> 0%
where the time goes in v1:
time: 1160 us
  waiting for transfers between devices  1010 us (87%)
  other arithmetic  52.6 us (5%)
  matrix products  42.3 us (4%)
  local copies, waits for them, and re-layouts  34.6 us (3%)
  between operations  13.7 us (1%)
    all_gather x2, waiting for transfers between devices, rounds_launch(): return lax.all_gather(local, a_name).sum(axis=0)  572 us
    reduce_scatter x4, waiting for transfers between devices, share_layers(): lax.psum_scatter(partial_sum, 'depth', scatter_dimension=1, tiled=True)  259 us
    all_gather x4, waiting for transfers between devices, multiply(): lax.all_gather(left_tile, 'col', axis=1, tiled=True)  107 us
    all_gather x2, waiting for transfers between devices, on_device(): lax.all_gather(operand, 'depth', axis=1, tiled=True)  71.9 us
    dot_general x4, matrix products, multiply(): jnp.dot(lax.all_gather(left_tile, 'col', axis=1, tiled=True), right_side,...  42.3 us
    mul x10, local copies, waits for them, and re-layouts, apply_mask(): values.reshape(row_count, BLK, col_count, BLK) * keep_mask[:, None, :, None]  32.2 us
    reduce_sum x2, other arithmetic, rounds_launch(): return lax.all_gather(local, a_name).sum(axis=0)  24.9 us
  transfers between devices with their start and end apart: 12, of which 12 were waited for; matrix products, arithmetic and copies ran while one was open for 5% of the time, Pallas kernels for 0%

profile of v1, /device:TPU:0, one launch (start us, length us, event | category | flops | bytes accessed | tf_op | source)
XLA Modules:
  0.0 1155.8 jit_solution(8255825628038279232)
XLA Ops:
  9.8 3.4 mul.84
  13.2 2.9 multiply_convert_fusion
  16.2 37.3 %all-gather.13.cloned.1.call-done = bf16[1024,2048]{1,0:T(8,128)(2,1)} async-done(((bf16[1024,512]{1,0:T(8,128)(2,1)}), bf16[1024,2048]{1,0:T(8,128)(2,1)}) %all-gather.13.cloned.1.call-update) | async-done | bytes 4194320 | tf_op jit(solution)/shard_map/all_gather | solution.py:60
  53.5 4.4 broadcast_select_fusion.1
  58.7 286.0 %all-gather.23.cloned.1.call-done = bf16[4096,2048]{1,0:T(8,128)(2,1)} async-done(((bf16[1024,2048]{1,0:T(8,128)(2,1)}), bf16[4096,2048]{1,0:T(8,128)(2,1)}) %all-gather.23.cloned.1.call-update) | async-done | bytes 16777232 | tf_op jit(solution)/shard_map/all_gather | solution.py:11
  344.7 12.4 %reduce_sum.24 = bf16[1024,2048]{1,0:T(8,128)(2,1)} reduce(bf16[4,1024,2048]{2,1,0:T(8,128)(2,1)} %bitcast.36, bf16[]{:T(256)} %constant.33.clone.1), dimensions={0}, to_apply=%region_0.1 | reduce | flops 6291456 | bytes 20971522 | tf_op jit(solution)/shard_map/reduce_sum | solution.py:11
  357.2 20.4 %all-gather.11.cloned.1.call-done = bf16[1024,1024]{1,0:T(8,128)(2,1)} async-done(((bf16[1024,512]{1,0:T(8,128)(2,1)}), bf16[1024,1024]{1,0:T(8,128)(2,1)}) %all-gather.11.cloned.1.call-update) | async-done | bytes 2097168 | tf_op jit(solution)/shard_map/all_gather | solution.py:47
  377.6 10.6 fusion.1
  389.3 2.3 mul.86
  391.6 3.6 mul.87
  395.2 64.9 %reduce-scatter.5.cloned.1.call-done = f32[1024,512]{1,0:T(8,128)} async-done(((f32[1024,2048]{1,0:T(8,128)}), f32[1024,512]{1,0:T(8,128)}) %reduce-scatter.5.cloned.1.call-update) | async-done | bytes 2097168 | tf_op jit(solution)/shard_map/reduce_scatter | solution.py:53
  460.1 2.9 multiply_convert_fusion.2
  463.1 33.2 %all-gather.15.cloned.1.call-done = bf16[1024,1024]{1,0:T(8,128)(2,1)} async-done(((bf16[1024,512]{1,0:T(8,128)(2,1)}), bf16[1024,1024]{1,0:T(8,128)(2,1)}) %all-gather.15.cloned.1.call-update) | async-done | bytes 2097168 | tf_op jit(solution)/shard_map/all_gather | solution.py:47
  496.3 10.6 fusion.2
  509.6 5.0 mul.91
  514.7 64.2 %reduce-scatter.7.cloned.1.call-done = f32[1024,512]{1,0:T(8,128)} async-done(((f32[1024,2048]{1,0:T(8,128)}), f32[1024,512]{1,0:T(8,128)}) %reduce-scatter.7.cloned.1.call-update) | async-done | bytes 2097168 | tf_op jit(solution)/shard_map/reduce_scatter | solution.py:53
  578.8 4.9 subtract_convert_fusion
  583.8 34.6 %all-gather.19.cloned.1.call-done = bf16[1024,2048]{1,0:T(8,128)(2,1)} async-done(((bf16[1024,512]{1,0:T(8,128)(2,1)}), bf16[1024,2048]{1,0:T(8,128)(2,1)}) %all-gather.19.cloned.1.call-update) | async-done | bytes 4194320 | tf_op jit(solution)/shard_map/all_gather | solution.py:60
  618.4 4.4 broadcast_select_fusion
  623.6 286.0 %all-gather.25.cloned.1.call-done = bf16[4096,2048]{1,0:T(8,128)(2,1)} async-done(((bf16[1024,2048]{1,0:T(8,128)(2,1)}), bf16[4096,2048]{1,0:T(8,128)(2,1)}) %all-gather.25.cloned.1.call-update) | async-done | bytes 16777232 | tf_op jit(solution)/shard_map/all_gather | solution.py:11
  909.6 12.4 %reduce_sum.25 = bf16[1024,2048]{1,0:T(8,128)(2,1)} reduce(bf16[4,1024,2048]{2,1,0:T(8,128)(2,1)} %bitcast.35, bf16[]{:T(256)} %constant.33.clone.1), dimensions={0}, to_apply=%region_3.4 | reduce | flops 6291456 | bytes 20971522 | tf_op jit(solution)/shard_map/reduce_sum | solution.py:11
  922.1 20.4 %all-gather.17.cloned.1.call-done = bf16[1024,1024]{1,0:T(8,128)(2,1)} async-done(((bf16[1024,512]{1,0:T(8,128)(2,1)}), bf16[1024,1024]{1,0:T(8,128)(2,1)}) %all-gather.17.cloned.1.call-update) | async-done | bytes 2097168 | tf_op jit(solution)/shard_map/all_gather | solution.py:47
  942.5 10.6 fusion.3
  953.4 2.3 mul.94
  955.7 3.6 mul.95
  959.3 65.8 %reduce-scatter.9.cloned.1.call-done = f32[1024,512]{1,0:T(8,128)} async-done(((f32[1024,2048]{1,0:T(8,128)}), f32[1024,512]{1,0:T(8,128)}) %reduce-scatter.9.cloned.1.call-update) | async-done | bytes 2097168 | tf_op jit(solution)/shard_map/reduce_scatter | solution.py:53
  1025.1 2.9 multiply_convert_fusion.1
  1028.3 33.0 %all-gather.21.cloned.1.call-done = bf16[1024,1024]{1,0:T(8,128)(2,1)} async-done(((bf16[1024,512]{1,0:T(8,128)(2,1)}), bf16[1024,1024]{1,0:T(8,128)(2,1)}) %all-gather.21.cloned.1.call-update) | async-done | bytes 2097168 | tf_op jit(solution)/shard_map/all_gather | solution.py:47
  1061.3 10.6 fusion.4
  1074.4 5.0 mul.99
  1079.4 64.4 %reduce-scatter.11.cloned.1.call-done = f32[1024,512]{1,0:T(8,128)} async-done(((f32[1024,2048]{1,0:T(8,128)}), f32[1024,512]{1,0:T(8,128)}) %reduce-scatter.11.cloned.1.call-update) | async-done | bytes 2097168 | tf_op jit(solution)/shard_map/reduce_scatter | solution.py:53
  1143.8 5.2 multiply_subtract_fusion
  (57 shorter events, 11.8 us)
Async XLA Ops:
  6.5 0.8 copy-start
  6.5 46.9 %all-gather.13.cloned.1.call-start = ((), (), s32[]{:S(2)}) async-start(), calls=%async_computation.5 | async-start | bytes 5242880 | tf_op jit(solution)/shard_map/all_gather | solution.py:60
  16.1 328.6 %all-gather.23.cloned.1.call-start = ((), (), s32[]{:S(2)}) async-start(), calls=%async_computation.14 | async-start | bytes 20971520 | tf_op jit(solution)/shard_map/all_gather | solution.py:11
  57.9 319.7 %all-gather.11.cloned.1.call-start = ((), (), s32[]{:S(2)}) async-start(), calls=%async_computation.4 | async-start | bytes 3145728 | tf_op jit(solution)/shard_map/all_gather | solution.py:47
  58.6 401.5 %reduce-scatter.5.cloned.1.call-start = ((), (), s32[]{:S(2)}) async-start(), calls=%async_computation.6 | async-start | bytes 10485760 | tf_op jit(solution)/shard_map/reduce_scatter | solution.py:53
  388.2 0.9 copy-start.2
  388.2 108.1 %all-gather.15.cloned.1.call-start = ((), (), s32[]{:S(2)}) async-start(), calls=%async_computation.7 | async-start | bytes 3145728 | tf_op jit(solution)/shard_map/all_gather | solution.py:47
  463.0 115.8 %reduce-scatter.7.cloned.1.call-start = ((), (), s32[]{:S(2)}) async-start(), calls=%async_computation.8 | async-start | bytes 10485760 | tf_op jit(solution)/shard_map/reduce_scatter | solution.py:53
  506.9 111.5 %all-gather.19.cloned.1.call-start = ((), (), s32[]{:S(2)}) async-start(), calls=%async_computation.10 | async-start | bytes 5242880 | tf_op jit(solution)/shard_map/all_gather | solution.py:60
  583.7 325.9 %all-gather.25.cloned.1.call-start = ((), (), s32[]{:S(2)}) async-start(), calls=%async_computation.15 | async-start | bytes 20971520 | tf_op jit(solution)/shard_map/all_gather | solution.py:11
  622.8 319.7 %all-gather.17.cloned.1.call-start = ((), (), s32[]{:S(2)}) async-start(), calls=%async_computation.9 | async-start | bytes 3145728 | tf_op jit(solution)/shard_map/all_gather | solution.py:47
  623.6 401.5 %reduce-scatter.9.cloned.1.call-start = ((), (), s32[]{:S(2)}) async-start(), calls=%async_computation.11 | async-start | bytes 10485760 | tf_op jit(solution)/shard_map/reduce_scatter | solution.py:53
  953.1 108.1 %all-gather.21.cloned.1.call-start = ((), (), s32[]{:S(2)}) async-start(), calls=%async_computation.12 | async-start | bytes 3145728 | tf_op jit(solution)/shard_map/all_gather | solution.py:47
  1028.0 115.8 %reduce-scatter.11.cloned.1.call-start = ((), (), s32[]{:S(2)}) async-start(), calls=%async_computation.13 | async-start | bytes 10485760 | tf_op jit(solution)/shard_map/reduce_scatter | solution.py:53
  1143.8 5.2 copy-start.1
Sparse Core Ops, SparseCore 0:
  16.2 37.1 all-gather.12
  58.0 286.6 all-gather.22
  346.3 31.2 all-gather.10
  388.3 71.7 reduce-scatter.4
  463.1 33.1 all-gather.14
  507.0 71.7 reduce-scatter.6
  583.9 34.4 all-gather.18
  622.9 286.6 all-gather.24
  911.2 31.2 all-gather.16
  953.3 71.7 reduce-scatter.8
  1028.1 33.1 all-gather.20
  1072.0 71.7 reduce-scatter.10
